TPU v7x, 32 devices: a whole 2x2x4 slice. The times are simulated.
32 devices in a mesh: groups: 2 (over y), tile: 4 (over x, core), cuts: 4 (over z).
Axes of the slice: x: 2, y: 2, z: 4, core: 2. Of those that a mesh axis runs over, the one named last changes fastest.
Arguments:
- trade: bfloat16 [16, 4, 256, 8192], P(('groups', 'cuts'), 'tile'), parts along dimension 0, may hold values from -6 to 6
- factor: bfloat16 [32768, 256], P(('groups', 'tile', 'cuts')), parts along dimension 0, may hold values from -0.375 to 0.375
- scales: float32 [16, 256], P(('groups', 'cuts')), parts along dimension 0, may hold values from 0.1 to 1.9
- core: float32 [512, 256], P('groups'), parts along dimension 0, may hold values from -4 to 4
Outputs:
- grad_factor: float32 [32768, 256], P(('groups', 'tile', 'cuts')), parts along dimension 0
- grad_window: float32 [1024, 256], P(('groups', 'cuts')), parts along dimension 0
- grad_core: float32 [512, 256], P('groups'), parts along dimension 0
- grad_scales: float32 [16, 256], P(('groups', 'cuts')), parts along dimension 0
There are 2 independent parts, one for each index of `groups`. A program takes and returns all parts, laid end to end along the dimension named above; each array names one. Nothing has to cross between parts.
All inputs are finite; a program needn't handle non-finite values.
Results may differ from a plain program's by a relative error of at most 0.00055.
Values may be sent and summed in bfloat16 or wider, within the bound.
A program may use at most 128 MiB of HBM per device.

v0:
```python
import math
import jax
import jax.numpy as jnp
from jax import lax
from jax.sharding import PartitionSpec as P

P_SIZE = 256


def swapped(value, axis, distance):
    mask = 2**distance
    pairs = [(source, source ^ mask) for source in range(lax.axis_size(axis))]
    return lax.ppermute(value, axis, pairs)


def from_root(block, axis, source):
    block = jnp.where(lax.axis_index(axis) == source, block, jnp.zeros_like(block))
    return lax.psum(block, axis)


def body(trade, factor, scales, core):
    n_cuts = lax.axis_size("cuts")
    band_index = lax.axis_index("tile") % 2
    months = trade.shape[0]
    rows_band = trade.shape[2]
    window_size = 2 * rows_band
    highest = lax.Precision.HIGHEST
    own_block = lax.all_gather(factor, "cuts", axis=0, tiled=True)
    block = own_block.shape[0]
    partner_block = swapped(own_block, "tile", 0)
    first_block = jnp.where(band_index == 0, own_block, partner_block)
    second_block = jnp.where(band_index == 0, partner_block, own_block)
    column_factor = jnp.concatenate([first_block, second_block], 0)
    window_block = from_root(own_block, "tile", 0)
    window_rows = lax.dynamic_slice_in_dim(window_block, band_index * rows_band, rows_band, 0)
    window32 = window_rows.astype(jnp.float32)
    coef = 1.0 / math.sqrt(months * n_cuts * window_size)
    acc_columns = jnp.zeros((2 * block, P_SIZE), jnp.float32)
    acc_window = jnp.zeros((rows_band, P_SIZE), jnp.float32)
    acc_core = jnp.zeros((P_SIZE, P_SIZE), jnp.float32)
    diag_terms = []
    for month in range(months):
        diag_k = scales[month]
        inner = diag_k[:, None] * core * diag_k[None, :]
        mapped = jnp.dot(window32, inner, precision=highest).astype(jnp.bfloat16)
        model = lax.dot_general(
            mapped, column_factor, (((1,), (1,)), ((), ())), preferred_element_type=jnp.float32
        )
        residual = (trade[month, 0].astype(jnp.float32) - model).astype(jnp.bfloat16)
        acc_columns = acc_columns + lax.dot_general(
            residual, mapped, (((0,), (0,)), ((), ())), preferred_element_type=jnp.float32
        )
        projected = jnp.dot(residual, column_factor, preferred_element_type=jnp.float32)
        acc_window = acc_window + jnp.dot(projected, inner.T, precision=highest)
        gram = jnp.dot(window32.T, projected, precision=highest)
        acc_core = acc_core + diag_k[:, None] * gram * diag_k[None, :]
        weighted = gram * core
        diag_terms.append(
            jnp.dot(weighted, diag_k, precision=highest)
            + jnp.dot(weighted.T, diag_k, precision=highest)
        )
    diag_stack = jnp.stack(diag_terms, 0)
    halves = acc_columns.reshape(2, block, P_SIZE)
    mine = jnp.where(band_index == 0, halves[0], halves[1])
    other = jnp.where(band_index == 0, halves[1], halves[0])
    received = swapped(other, "tile", 0)
    grad_factor = lax.psum_scatter(mine + received, "cuts", scatter_dimension=0, tiled=True)
    padded = lax.dynamic_update_slice_in_dim(
        jnp.zeros((window_size, P_SIZE), jnp.float32), acc_window, band_index * rows_band, 0
    )
    window_part = lax.psum_scatter(padded, "cuts", scatter_dimension=0, tiled=True)
    window_total = lax.psum(window_part, "tile")
    core_total = lax.psum(acc_core, ("tile", "cuts"))
    diag_total = lax.psum(diag_stack, "tile")
    return (-coef * grad_factor, -coef * window_total, -coef * core_total, -coef * diag_total)


def solution(mesh):
    return jax.shard_map(
        body,
        mesh=mesh,
        in_specs=(
            P(("groups", "cuts"), "tile", None, None),
            P(("groups", "tile", "cuts"), None),
            P(("groups", "cuts"), None),
            P("groups", None),
        ),
        out_specs=(
            P(("groups", "tile", "cuts"), None),
            P(("groups", "cuts"), None),
            P("groups", None),
            P(("groups", "cuts"), None),
        ),
        check_vma=False,
    )
```

profile of v0, /device:TPU:0, one launch (start us, length us, event | category | flops | bytes accessed | tf_op | source)
XLA Modules:
  0.0 385.2 jit_solution(4281532647967686441)
XLA Ops:
  7.2 0.7 all-gather.2.cloned.1.call-update
  7.9 50.3 %all-gather.2.cloned.1.call-done = bf16[4096,256]{1,0:T(8,128)(2,1)} async-done(((bf16[1024,256]{1,0:T(8,128)(2,1)}), bf16[4096,256]{1,0:T(8,128)(2,1)}) %all-gather.2.cloned.1.call-update) | async-done | bytes 2097168 | tf_op jit(solution)/shard_map/all_gather | solution.py:28
  58.2 4.5 %collective-permute-done = bf16[4096,256]{1,0:T(8,128)(2,1)} collective-permute-done((bf16[4096,256]{1,0:T(8,128)(2,1)}, bf16[4096,256]{1,0:T(8,128)(2,1)}, u32[]{:S(2)}, u32[]{:S(2)}) %collective-permute-start) | collective-permute-done | bytes 2097184 | tf_op jit(solution)/shard_map/ppermute | solution.py:13
  62.7 4.6 %broadcast_select_fusion.2 = (bf16[4096,256]{1,0:T(8,128)(2,1)S(1)}, bf16[4096,256]{1,0:T(8,128)(2,1)}, bf16[4096,256]{1,0:T(8,128)(2,1)}) fusion(bf16[4096,256]{1,0:T(8,128)(2,1)} %all-gather.2.cloned.1.call-done, bf16[4096,256]{1,0:T(8,128)(2,1)} %collective-permute-done, pred[]{:T(512)S(6)} %eq.6, pred[]{:T(512)S(6)} %eq.12), kind=kLoop, calls=%fused_computation.10 | loop fusion | flops 3145728 | bytes 10485762 | tf_op jit(solution)/shard_map/jit(_where)/select_n | solution.py:31
  67.5 50.2 %all-reduce.4.cloned.1.call-done = bf16[4096,256]{1,0:T(8,128)(2,1)} async-done(((bf16[4096,256]{1,0:T(8,128)(2,1)}), bf16[4096,256]{1,0:T(8,128)(2,1)}) %all-reduce.4.cloned.1.call-update) | async-done | bytes 2097168 | tf_op jit(solution)/shard_map/psum | solution.py:18
  117.6 1.3 convolution_convert_fusion.1
  119.0 4.3 %fusion = bf16[256,8192]{1,0:T(8,128)(2,1)S(1)} fusion(bf16[256,256]{1,0:T(8,128)(2,1)S(1)} %convolution_convert_fusion.1, bf16[2,1,256,8192]{3,2,1,0:T(8,128)(2,1)} %param.4, bf16[4096,256]{1,0:T(8,128)(2,1)} %get-tuple-element.5, bf16[4096,256]{1,0:T(8,128)(2,1)S(1)} %get-tuple-element.4), kind=kOutput, calls=%fused_computation.3 | convolution fusion | flops 1088421888 | bytes 12713984 | tf_op jit(solution)/shard_map/dot_general | solution.py:46
  123.2 1.5 convolution_convert_fusion
  124.7 9.6 %fusion.1 = bf16[256,8192]{1,0:T(8,128)(2,1)S(1)} fusion(bf16[256,256]{1,0:T(8,128)(2,1)S(1)} %convolution_convert_fusion, bf16[2,1,256,8192]{3,2,1,0:T(8,128)(2,1)} %param.4, bf16[4096,256]{1,0:T(8,128)(2,1)S(1)} %copy-done.6, bf16[4096,256]{1,0:T(8,128)(2,1)S(1)} %get-tuple-element.4), kind=kOutput, calls=%fused_computation.4 | convolution fusion | flops 1088421888 | bytes 12713984 | tf_op jit(solution)/shard_map/dot_general | solution.py:46
  134.4 1.3 fusion.43
  135.7 0.6 copy-done.2
  136.3 1.3 convolution_add_fusion
  137.7 2.8 slice_select_fusion
  140.5 1.6 copy-done
  142.2 4.2 %fusion.41 = f32[256,256]{1,0:T(8,128)S(1)} fusion(bf16[256,8192]{1,0:T(8,128)(2,1)} %copy-done.4, bf16[4096,256]{1,0:T(8,128)(2,1)} %get-tuple-element.5, bf16[4096,256]{1,0:T(8,128)(2,1)S(1)} %get-tuple-element.4), kind=kOutput, calls=%fused_computation.61 | convolution fusion | flops 1082130432 | bytes 8650752 | tf_op jit(solution)/shard_map/dot_general | solution.py:53
  146.4 0.5 fusion.7
  146.9 1.2 fusion.40
  148.2 0.5 fusion.2
  148.7 0.8 copy-done.5
  149.6 1.2 fusion.24
  150.8 1.9 multiply_add_fusion
  152.8 18.8 %reduce-scatter.5.cloned.1.call-done = f32[128,256]{1,0:T(8,128)} async-done(((f32[512,256]{1,0:T(8,128)}), f32[128,256]{1,0:T(8,128)}) %reduce-scatter.5.cloned.1.call-update) | async-done | bytes 131088 | tf_op jit(solution)/shard_map/reduce_scatter | solution.py:71
  171.7 7.4 %select_add_fusion = f32[4096,256]{1,0:T(8,128)} fusion(f32[4096,256]{1,0:T(8,128)} %collective-permute-done.1, f32[8192,256]{1,0:T(8,128)} %copy-done, pred[]{:T(512)S(6)} %eq.6), kind=kLoop, calls=%fused_computation.6 | loop fusion | flops 2097152 | bytes 16777216 | tf_op jit(solution)/shard_map/add | solution.py:67
  179.6 0.3 fusion.17
  180.3 5.7 %psum.31 = f32[2,256]{1,0:T(2,128)S(1)} all-reduce(f32[2,256]{1,0:T(2,128)S(1)} %pad_maximum_fusion.1), channel_id=1, replica_groups=mesh['groups'=2,'tile'=4,'cuts'=4] {'tile'}, use_global_device_ids=true, to_apply=%region_5.6 | all-reduce | flops 512 | bytes 4096 | tf_op jit(solution)/shard_map/psum | solution.py:74
  185.9 0.6 broadcast_multiply_fusion.3
  186.5 76.4 %all-reduce.8.cloned.1.call-done = f32[256,256]{1,0:T(8,128)} async-done(((f32[256,256]{1,0:T(8,128)}), f32[256,256]{1,0:T(8,128)}) %all-reduce.8.cloned.1.call-update) | async-done | bytes 262160 | tf_op jit(solution)/shard_map/psum | solution.py:73
  262.9 1.7 broadcast_multiply_fusion.1
  264.6 32.5 %all-reduce.6.cloned.1.call-done = f32[128,256]{1,0:T(8,128)} async-done(((f32[128,256]{1,0:T(8,128)}), f32[128,256]{1,0:T(8,128)}) %all-reduce.6.cloned.1.call-update) | async-done | bytes 131088 | tf_op jit(solution)/shard_map/psum | solution.py:72
  297.1 1.6 broadcast_multiply_fusion.2
  298.7 77.4 %reduce-scatter.3.cloned.1.call-done = f32[1024,256]{1,0:T(8,128)} async-done(((f32[4096,256]{1,0:T(8,128)}), f32[1024,256]{1,0:T(8,128)}) %reduce-scatter.3.cloned.1.call-update) | async-done | bytes 1048592 | tf_op jit(solution)/shard_map/reduce_scatter | solution.py:67
  376.1 2.3 broadcast_multiply_fusion
  (37 shorter events, 1.3 us)
Async XLA Ops:
  7.2 51.1 %all-gather.2.cloned.1.call-start = ((), (), s32[]{:S(2)}) async-start(), calls=%async_computation.2 | async-start | bytes 2621440 | tf_op jit(solution)/shard_map/all_gather | solution.py:28
  7.9 109.7 %all-reduce.4.cloned.1.call-start = ((), (), s32[]{:S(2)}) async-start(), calls=%async_computation.3 | async-start | bytes 4194304 | tf_op jit(solution)/shard_map/psum | solution.py:18
  58.2 4.5 %collective-permute-start = (bf16[4096,256]{1,0:T(8,128)(2,1)}, bf16[4096,256]{1,0:T(8,128)(2,1)}, u32[]{:S(2)}, u32[]{:S(2)}) collective-permute-start(bf16[4096,256]{1,0:T(8,128)(2,1)} %all-gather.2.cloned.1.call-done), channel_id=1, source_target_pairs={{0,4},{4,0},{8,12},{12,8},{1,5},{5,1},{9,13},{13,9},{2,6},{6,2},{1... | collective-permute-start | bytes 6291464 | tf_op jit(solution)/shard_map/ppermute | solution.py:13
  58.2 9.2 %copy-start.8 = (f32[2,256]{1,0:T(2,128)S(1)}, f32[2,256]{1,0:T(2,128)}, u32[]{:S(2)}) copy-start(f32[2,256]{1,0:T(2,128)} %param.6) | copy-start | bytes 6148
  58.2 59.4 %copy-start.1 = (f32[256,256]{1,0:T(8,128)S(1)}, f32[256,256]{1,0:T(8,128)}, u32[]{:S(2)}) copy-start(f32[256,256]{1,0:T(8,128)} %param.7) | copy-start | bytes 786436
  67.4 104.2 %reduce-scatter.5.cloned.1.call-start = ((), (), s32[]{:S(2)}) async-start(), calls=%async_computation.5 | async-start | bytes 655360 | tf_op jit(solution)/shard_map/reduce_scatter | solution.py:71
  118.9 5.8 %copy-start.6 = (bf16[4096,256]{1,0:T(8,128)(2,1)S(1)}, bf16[4096,256]{1,0:T(8,128)(2,1)}, u32[]{:S(2)}) copy-start(bf16[4096,256]{1,0:T(8,128)(2,1)} %get-tuple-element.5) | copy-start | bytes 6291460
  123.2 11.1 %copy-start.4 = (bf16[256,8192]{1,0:T(8,128)(2,1)}, bf16[256,8192]{1,0:T(8,128)(2,1)S(1)}, u32[]{:S(2)}) copy-start(bf16[256,8192]{1,0:T(8,128)(2,1)S(1)} %fusion) | copy-start | bytes 12582916
  134.4 2.0 copy-start.2
  137.7 4.5 %copy-start = (f32[8192,256]{1,0:T(8,128)}, f32[8192,256]{1,0:T(8,128)S(1)}, u32[]{:S(2)}) copy-start(f32[8192,256]{1,0:T(8,128)S(1)} %convolution_add_fusion) | copy-start | bytes 25165828
  142.2 29.5 %collective-permute-start.1 = (f32[4096,256]{1,0:T(8,128)}, f32[4096,256]{1,0:T(8,128)}, u32[]{:S(2)}, u32[]{:S(2)}) collective-permute-start(f32[4096,256]{1,0:T(8,128)} %slice_select_fusion), channel_id=1, source_target_pairs={{0,4},{4,0},{8,12},{12,8},{1,5},{5,1},{9,13},{13,9},{2,6},{6,2},{1... | collective-permute-start | bytes 12582920 | tf_op jit(solution)/shard_map/ppermute | solution.py:13
  142.2 4.7 %copy-start.3 = (bf16[256,8192]{1,0:T(8,128)(2,1)S(1)}, bf16[256,8192]{1,0:T(8,128)(2,1)}, u32[]{:S(2)}) copy-start(bf16[256,8192]{1,0:T(8,128)(2,1)} %copy-done.2) | copy-start | bytes 12582916
  142.2 4.8 %copy-start.7 = (bf16[4096,256]{1,0:T(8,128)(2,1)S(1)}, bf16[4096,256]{1,0:T(8,128)(2,1)}, u32[]{:S(2)}) copy-start(bf16[4096,256]{1,0:T(8,128)(2,1)} %get-tuple-element.5) | copy-start | bytes 6291460
  148.7 0.8 copy-start.5
  149.5 113.4 %all-reduce.8.cloned.1.call-start = ((), (), s32[]{:S(2)}) async-start(), calls=%async_computation.7 | async-start | bytes 524288 | tf_op jit(solution)/shard_map/psum | solution.py:73
  152.8 144.3 %all-reduce.6.cloned.1.call-start = ((), (), s32[]{:S(2)}) async-start(), calls=%async_computation.6 | async-start | bytes 262144 | tf_op jit(solution)/shard_map/psum | solution.py:72
  171.6 204.5 %reduce-scatter.3.cloned.1.call-start = ((), (), s32[]{:S(2)}) async-start(), calls=%async_computation.4 | async-start | bytes 5242880 | tf_op jit(solution)/shard_map/reduce_scatter | solution.py:67
Sparse Core Ops, SparseCore 0:
  9.6 48.6 all-gather.1
  67.5 50.0 all-reduce.3
  149.7 21.8 reduce-scatter.4
  175.8 87.1 all-reduce.7
  265.2 31.8 all-reduce.5
  299.3 76.7 reduce-scatter.2
where the time goes:
time: 385 us
  waiting for transfers between devices  311 us (81%)
  matrix products  30 us (8%)
  other arithmetic  21 us (5%)
  between operations  14.3 us (4%)
  blocking collectives  5.67 us (1%)
    reduce_scatter x1, waiting for transfers between devices, body(): lax.psum_scatter(mine + received, 'cuts', scatter_dimension=0, tiled=True)  77.4 us
    psum x1, waiting for transfers between devices, body(): core_total = lax.psum(acc_core, ('tile', 'cuts'))  76.4 us
    all_gather x1, waiting for transfers between devices, body(): own_block = lax.all_gather(factor, 'cuts', axis=0, tiled=True)  50.3 us
    psum x1, waiting for transfers between devices, from_root(): return lax.psum(block, axis)  50.2 us
    psum x1, waiting for transfers between devices, body(): window_total = lax.psum(window_part, 'tile')  32.5 us
    reduce_scatter x1, waiting for transfers between devices, body(): lax.psum_scatter(padded, 'cuts', scatter_dimension=0, tiled=True)  18.8 us
    dot_general x2, matrix products, body(): lax.dot_general(mapped, column_factor, (((1,), (1,)), ((), ())), preferre...  13.9 us
  transfers between devices with their start and end apart: 8, of which 7 were waited for; matrix products, arithmetic and copies ran while one was open for 6% of the time, Pallas kernels for 0%

commit v1 on v0

--- a/solution.py
+++ b/solution.py
@@ -69,7 +69,8 @@
         jnp.zeros((window_size, P_SIZE), jnp.float32), acc_window, band_index * rows_band, 0
     )
     window_part = lax.psum_scatter(padded, "cuts", scatter_dimension=0, tiled=True)
-    window_total = lax.psum(window_part, "tile")
+    long_array = lax.all_gather(window_part, axis_name="tile")
+    window_total = jnp.sum(long_array, axis=0)
     core_total = lax.psum(acc_core, ("tile", "cuts"))
     diag_total = lax.psum(diag_stack, "tile")
     return (-coef * grad_factor, -coef * window_total, -coef * core_total, -coef * diag_total)

time: 385 us -> 351 us (0.912)
  waiting for transfers between devices: 311 us -> 270 us
  blocking collectives: 5.67 us -> 13.8 us
    psum x1 -> x0, waiting for transfers between devices: 32.5 us -> none  [body(): window_total = lax.psum(window_part, 'tile')]
    reduce_scatter x1, waiting for transfers between devices: 77.4 us -> 69.4 us  [body(): lax.psum_scatter(mine + received, 'cuts', scatter_dimension=0, tiled=True)]
    all_gather x0 -> x1, blocking collectives: none -> 7.22 us  [body(): long_array = lax.all_gather(window_part, axis_name='tile')]
    psum x1, waiting for transfers between devices: 76.4 us -> 71.2 us  [body(): core_total = lax.psum(acc_core, ('tile', 'cuts'))]
    reduce_scatter x1, waiting for transfers between devices: 18.8 us -> 23.3 us  [body(): lax.psum_scatter(padded, 'cuts', scatter_dimension=0, tiled=True)]
  transfers between devices with their start and end apart: 8 -> 7, of which waited for: 7 -> 6; matrix products, arithmetic and copies ran while one was open for 6% -> 6% of each run, Pallas kernels for 0% -> 0%
where the time goes in v1:
time: 351 us
  waiting for transfers between devices  270 us (77%)
  matrix products  29.8 us (8%)
  other arithmetic  20.1 us (6%)
  between operations  14 us (4%)
  blocking collectives  13.8 us (4%)
    psum x1, waiting for transfers between devices, body(): core_total = lax.psum(acc_core, ('tile', 'cuts'))  71.2 us
    reduce_scatter x1, waiting for transfers between devices, body(): lax.psum_scatter(mine + received, 'cuts', scatter_dimension=0, tiled=True)  69.4 us
    all_gather x1, waiting for transfers between devices, body(): own_block = lax.all_gather(factor, 'cuts', axis=0, tiled=True)  50.3 us
    psum x1, waiting for transfers between devices, from_root(): return lax.psum(block, axis)  50.2 us
    reduce_scatter x1, waiting for transfers between devices, body(): lax.psum_scatter(padded, 'cuts', scatter_dimension=0, tiled=True)  23.3 us
    dot_general x2, matrix products, body(): lax.dot_general(mapped, column_factor, (((1,), (1,)), ((), ())), preferre...  13.7 us
    add x1, other arithmetic, body(): mine + received  7.43 us
    all_gather x1, blocking collectives, body(): long_array = lax.all_gather(window_part, axis_name='tile')  7.22 us
  transfers between devices with their start and end apart: 7, of which 6 were waited for; matrix products, arithmetic and copies ran while one was open for 6% of the time, Pallas kernels for 0%

profile of v1, /device:TPU:0, one launch (start us, length us, event | category | flops | bytes accessed | tf_op | source)
XLA Modules:
  0.0 351.0 jit_solution(10740695266044333695)
XLA Ops:
  7.2 0.7 all-gather.3.cloned.1.call-update
  7.9 50.3 %all-gather.3.cloned.1.call-done = bf16[4096,256]{1,0:T(8,128)(2,1)} async-done(((bf16[1024,256]{1,0:T(8,128)(2,1)}), bf16[4096,256]{1,0:T(8,128)(2,1)}) %all-gather.3.cloned.1.call-update) | async-done | bytes 2097168 | tf_op jit(solution)/shard_map/all_gather | solution.py:28
  58.2 4.5 %collective-permute-done = bf16[4096,256]{1,0:T(8,128)(2,1)} collective-permute-done((bf16[4096,256]{1,0:T(8,128)(2,1)}, bf16[4096,256]{1,0:T(8,128)(2,1)}, u32[]{:S(2)}, u32[]{:S(2)}) %collective-permute-start) | collective-permute-done | bytes 2097184 | tf_op jit(solution)/shard_map/ppermute | solution.py:13
  62.7 4.6 %broadcast_select_fusion.2 = (bf16[4096,256]{1,0:T(8,128)(2,1)S(1)}, bf16[4096,256]{1,0:T(8,128)(2,1)}, bf16[4096,256]{1,0:T(8,128)(2,1)}) fusion(bf16[4096,256]{1,0:T(8,128)(2,1)} %all-gather.3.cloned.1.call-done, bf16[4096,256]{1,0:T(8,128)(2,1)} %collective-permute-done, pred[]{:T(512)S(6)} %eq.6, pred[]{:T(512)S(6)} %eq.12), kind=kLoop, calls=%fused_computation.10 | loop fusion | flops 3145728 | bytes 10485762 | tf_op jit(solution)/shard_map/jit(_where)/select_n | solution.py:31
  67.5 50.2 %all-reduce.3.cloned.1.call-done = bf16[4096,256]{1,0:T(8,128)(2,1)} async-done(((bf16[4096,256]{1,0:T(8,128)(2,1)}), bf16[4096,256]{1,0:T(8,128)(2,1)}) %all-reduce.3.cloned.1.call-update) | async-done | bytes 2097168 | tf_op jit(solution)/shard_map/psum | solution.py:18
  117.6 1.3 convolution_convert_fusion.1
  118.9 4.3 %fusion = bf16[256,8192]{1,0:T(8,128)(2,1)S(1)} fusion(bf16[256,256]{1,0:T(8,128)(2,1)S(1)} %convolution_convert_fusion.1, bf16[2,1,256,8192]{3,2,1,0:T(8,128)(2,1)} %param.4, bf16[4096,256]{1,0:T(8,128)(2,1)} %get-tuple-element.5, bf16[4096,256]{1,0:T(8,128)(2,1)S(1)} %get-tuple-element.4), kind=kOutput, calls=%fused_computation.3 | convolution fusion | flops 1088421888 | bytes 12713984 | tf_op jit(solution)/shard_map/dot_general | solution.py:46
  123.2 1.5 convolution_convert_fusion
  124.7 9.4 %fusion.1 = bf16[256,8192]{1,0:T(8,128)(2,1)S(1)} fusion(bf16[256,256]{1,0:T(8,128)(2,1)S(1)} %convolution_convert_fusion, bf16[2,1,256,8192]{3,2,1,0:T(8,128)(2,1)} %param.4, bf16[4096,256]{1,0:T(8,128)(2,1)S(1)} %copy-done.6, bf16[4096,256]{1,0:T(8,128)(2,1)S(1)} %get-tuple-element.4), kind=kOutput, calls=%fused_computation.4 | convolution fusion | flops 1088421888 | bytes 12713984 | tf_op jit(solution)/shard_map/dot_general | solution.py:46
  134.2 1.3 fusion.43
  135.5 0.6 copy-done.2
  136.1 1.3 convolution_add_fusion
  137.5 2.8 slice_select_fusion
  140.3 1.6 copy-done
  142.0 4.2 %fusion.41 = f32[256,256]{1,0:T(8,128)S(1)} fusion(bf16[256,8192]{1,0:T(8,128)(2,1)} %copy-done.4, bf16[4096,256]{1,0:T(8,128)(2,1)} %get-tuple-element.5, bf16[4096,256]{1,0:T(8,128)(2,1)S(1)} %get-tuple-element.4), kind=kOutput, calls=%fused_computation.61 | convolution fusion | flops 1082130432 | bytes 8650752 | tf_op jit(solution)/shard_map/dot_general | solution.py:53
  146.2 1.2 fusion.24
  147.5 1.2 fusion.40
  148.7 1.9 multiply_add_fusion
  150.9 0.5 fusion.7
  151.4 0.5 fusion.2
  152.0 0.8 copy-done.5
  152.8 7.4 %select_add_fusion = f32[4096,256]{1,0:T(8,128)} fusion(f32[4096,256]{1,0:T(8,128)} %collective-permute-done.1, f32[8192,256]{1,0:T(8,128)} %copy-done, pred[]{:T(512)S(6)} %eq.6), kind=kLoop, calls=%fused_computation.6 | loop fusion | flops 2097152 | bytes 16777216 | tf_op jit(solution)/shard_map/add | solution.py:67
  160.8 0.3 fusion.17
  161.5 6.6 %psum.23 = f32[2,256]{1,0:T(2,128)S(1)} all-reduce(f32[2,256]{1,0:T(2,128)S(1)} %pad_maximum_fusion.1), channel_id=1, replica_groups=mesh['groups'=2,'tile'=4,'cuts'=4] {'tile'}, use_global_device_ids=true, to_apply=%region_5.6 | all-reduce | flops 512 | bytes 4096 | tf_op jit(solution)/shard_map/psum | solution.py:75
  168.1 0.6 broadcast_multiply_fusion.3
  168.6 71.2 %all-reduce.5.cloned.1.call-done = f32[256,256]{1,0:T(8,128)} async-done(((f32[256,256]{1,0:T(8,128)}), f32[256,256]{1,0:T(8,128)}) %all-reduce.5.cloned.1.call-update) | async-done | bytes 262160 | tf_op jit(solution)/shard_map/psum | solution.py:74
  239.9 1.7 broadcast_multiply_fusion.1
  241.6 23.3 %reduce-scatter.5.cloned.1.call-done = f32[128,256]{1,0:T(8,128)} async-done(((f32[512,256]{1,0:T(8,128)}), f32[128,256]{1,0:T(8,128)}) %reduce-scatter.5.cloned.1.call-update) | async-done | bytes 131088 | tf_op jit(solution)/shard_map/reduce_scatter | solution.py:71
  264.9 7.2 %all-gather = f32[512,256]{1,0:T(8,128)S(1)} all-gather(f32[128,256]{1,0:T(8,128)} %reduce-scatter.5.cloned.1.call-done), channel_id=2, replica_groups=mesh['groups'=2,'tile'=4,'cuts'=4] {'tile'}, dimensions={0}, use_global_device_ids=true | all-gather | bytes 655360 | tf_op jit(solution)/shard_map/all_gather | solution.py:72
  272.2 0.7 broadcast_multiply_fusion.2
  272.8 69.4 %reduce-scatter.3.cloned.1.call-done = f32[1024,256]{1,0:T(8,128)} async-done(((f32[4096,256]{1,0:T(8,128)}), f32[1024,256]{1,0:T(8,128)}) %reduce-scatter.3.cloned.1.call-update) | async-done | bytes 1048592 | tf_op jit(solution)/shard_map/reduce_scatter | solution.py:67
  342.3 2.3 broadcast_multiply_fusion
  (36 shorter events, 1.4 us)
Async XLA Ops:
  7.2 51.1 %all-gather.3.cloned.1.call-start = ((), (), s32[]{:S(2)}) async-start(), calls=%async_computation.2 | async-start | bytes 2621440 | tf_op jit(solution)/shard_map/all_gather | solution.py:28
  7.9 109.7 %all-reduce.3.cloned.1.call-start = ((), (), s32[]{:S(2)}) async-start(), calls=%async_computation.3 | async-start | bytes 4194304 | tf_op jit(solution)/shard_map/psum | solution.py:18
  58.2 4.5 %collective-permute-start = (bf16[4096,256]{1,0:T(8,128)(2,1)}, bf16[4096,256]{1,0:T(8,128)(2,1)}, u32[]{:S(2)}, u32[]{:S(2)}) collective-permute-start(bf16[4096,256]{1,0:T(8,128)(2,1)} %all-gather.3.cloned.1.call-done), channel_id=1, source_target_pairs={{0,4},{4,0},{8,12},{12,8},{1,5},{5,1},{9,13},{13,9},{2,6},{6,2},{1... | collective-permute-start | bytes 6291464 | tf_op jit(solution)/shard_map/ppermute | solution.py:13
  58.2 9.2 %copy-start.8 = (f32[2,256]{1,0:T(2,128)S(1)}, f32[2,256]{1,0:T(2,128)}, u32[]{:S(2)}) copy-start(f32[2,256]{1,0:T(2,128)} %param.6) | copy-start | bytes 6148
  58.2 59.4 %copy-start.1 = (f32[256,256]{1,0:T(8,128)S(1)}, f32[256,256]{1,0:T(8,128)}, u32[]{:S(2)}) copy-start(f32[256,256]{1,0:T(8,128)} %param.7) | copy-start | bytes 786436
  67.4 172.5 %all-reduce.5.cloned.1.call-start = ((), (), s32[]{:S(2)}) async-start(), calls=%async_computation.6 | async-start | bytes 524288 | tf_op jit(solution)/shard_map/psum | solution.py:74
  118.9 5.8 %copy-start.6 = (bf16[4096,256]{1,0:T(8,128)(2,1)S(1)}, bf16[4096,256]{1,0:T(8,128)(2,1)}, u32[]{:S(2)}) copy-start(bf16[4096,256]{1,0:T(8,128)(2,1)} %get-tuple-element.5) | copy-start | bytes 6291460
  123.2 10.9 %copy-start.4 = (bf16[256,8192]{1,0:T(8,128)(2,1)}, bf16[256,8192]{1,0:T(8,128)(2,1)S(1)}, u32[]{:S(2)}) copy-start(bf16[256,8192]{1,0:T(8,128)(2,1)S(1)} %fusion) | copy-start | bytes 12582916
  134.2 2.0 copy-start.2
  137.5 4.5 %copy-start = (f32[8192,256]{1,0:T(8,128)}, f32[8192,256]{1,0:T(8,128)S(1)}, u32[]{:S(2)}) copy-start(f32[8192,256]{1,0:T(8,128)S(1)} %convolution_add_fusion) | copy-start | bytes 25165828
  142.0 10.9 %collective-permute-start.1 = (f32[4096,256]{1,0:T(8,128)}, f32[4096,256]{1,0:T(8,128)}, u32[]{:S(2)}, u32[]{:S(2)}) collective-permute-start(f32[4096,256]{1,0:T(8,128)} %slice_select_fusion), channel_id=1, source_target_pairs={{0,4},{4,0},{8,12},{12,8},{1,5},{5,1},{9,13},{13,9},{2,6},{6,2},{1... | collective-permute-start | bytes 12582920 | tf_op jit(solution)/shard_map/ppermute | solution.py:13
  142.0 5.5 %copy-start.3 = (bf16[256,8192]{1,0:T(8,128)(2,1)S(1)}, bf16[256,8192]{1,0:T(8,128)(2,1)}, u32[]{:S(2)}) copy-start(bf16[256,8192]{1,0:T(8,128)(2,1)} %copy-done.2) | copy-start | bytes 12582916
  142.0 5.5 %copy-start.7 = (bf16[4096,256]{1,0:T(8,128)(2,1)S(1)}, bf16[4096,256]{1,0:T(8,128)(2,1)}, u32[]{:S(2)}) copy-start(bf16[4096,256]{1,0:T(8,128)(2,1)} %get-tuple-element.5) | copy-start | bytes 6291460
  150.7 114.2 %reduce-scatter.5.cloned.1.call-start = ((), (), s32[]{:S(2)}) async-start(), calls=%async_computation.5 | async-start | bytes 655360 | tf_op jit(solution)/shard_map/reduce_scatter | solution.py:71
  151.9 0.8 copy-start.5
  152.8 189.5 %reduce-scatter.3.cloned.1.call-start = ((), (), s32[]{:S(2)}) async-start(), calls=%async_computation.4 | async-start | bytes 5242880 | tf_op jit(solution)/shard_map/reduce_scatter | solution.py:67
Sparse Core Ops, SparseCore 0:
  9.6 48.6 all-gather.2
  67.5 50.0 all-reduce.2
  150.8 89.0 all-reduce.4
  242.7 22.1 reduce-scatter.4
  267.1 75.0 reduce-scatter.2
